TPU v7x, 32 devices: a whole 2x2x4 slice. The times are simulated.
32 devices in a mesh: groups: 2 (over x), rows: 16 (over z, y, core).
Axes of the slice: x: 2, y: 2, z: 4, core: 2. Of those that a mesh axis runs over, the one named last changes fastest.
Arguments:
- image_query: bfloat16 [12288, 2048], P(('groups', 'rows')), parts along dimension 0, may hold values from -40 to 40
- image_pairs: bfloat16 [2, 12288, 2048], P(None, ('groups', 'rows')), parts along dimension 1, may hold values from -6 to 6
- text_query: bfloat16 [512, 2048], P(('groups', 'rows')), parts along dimension 0, may hold values from -40 to 40
- text_pairs: bfloat16 [2, 512, 2048], P(None, ('groups', 'rows')), parts along dimension 1, may hold values from -6 to 6
- text_mask: int32 [512], P('groups'), parts along dimension 0, may hold values 0 or 1
- window_offsets: int32 [16, 2], replicated, may hold values from -1 to 1, as said below
- timestep: int32 [1], replicated, may hold values from 0 to 49
- gate_table: float32 [50, 2, 2048], replicated, may hold values from 0.5 to 2
Outputs:
- image_out: bfloat16 [12288, 2048], P(('groups', 'rows')), parts along dimension 0
- text_out: bfloat16 [512, 2048], P(('groups', 'rows')), parts along dimension 0
There are 2 independent parts, one for each index of `groups`. A program takes and returns all parts, laid end to end along the dimension named above; an argument that names none is the same for every part. Nothing has to cross between parts.
Inputs may be any that keep to these rules, and one draw needn't show every extreme that they name: window_offsets[h, 0] is -1 or 0 and window_offsets[h, 1] is 0 or 1; some head has -1 and some head has 1.
All inputs are finite; a program needn't handle non-finite values.
Results may differ from a plain program's by a relative error of at most 0.02.
Values may be sent and summed in bfloat16 or wider, within the bound.
A program may use at most 128 MiB of HBM per device.

v0:
```python
import math
import jax
import jax.numpy as jnp
from jax import lax
from jax.sharding import PartitionSpec as P

TILE = 384
masked_score = -1e30


def extended_2(cells, sides, width):
    for axis, dim in sides:
        count = lax.axis_size(axis)
        ends = count - 1
        head = lax.slice_in_dim(cells, 0, width, axis=dim)
        tail = lax.slice_in_dim(cells, cells.shape[dim] - width, cells.shape[dim], axis=dim)
        cells = jnp.concatenate(
            [
                lax.ppermute(tail, axis, [(i, (i + 1) % count) for i in range(ends)]),
                cells,
                lax.ppermute(head, axis, [((i + 1) % count, i) for i in range(ends)]),
            ],
            axis=dim,
        )
    return cells


def attend_tiles(queries, key_rows, value_rows, allowed, scaling):
    scores = (
        jnp.einsum("tqhe,tkhe->tqhk", queries, key_rows, preferred_element_type=jnp.float32)
        * scaling
    )
    scores = jnp.where(allowed, scores, masked_score)
    maxima = jnp.max(scores, axis=-1)
    exponent = jnp.where(allowed, jnp.exp(scores - maxima[..., None]), 0.0)
    totals = jnp.sum(exponent, axis=-1)
    summed = jnp.einsum(
        "tqhk,tkhe->tqhe",
        exponent.astype(jnp.bfloat16),
        value_rows,
        preferred_element_type=jnp.float32,
    )
    return (maxima, totals, summed.astype(jnp.bfloat16))


def attend_rows(queries, key_rows, value_rows, allowed, scaling):
    scores = (
        jnp.einsum("qhe,khe->qhk", queries, key_rows, preferred_element_type=jnp.float32) * scaling
    )
    scores = jnp.where(allowed, scores, masked_score)
    maxima = jnp.max(scores, axis=-1)
    exponent = jnp.where(allowed, jnp.exp(scores - maxima[..., None]), 0.0)
    totals = jnp.sum(exponent, axis=-1)
    summed = jnp.einsum(
        "qhk,khe->qhe",
        exponent.astype(jnp.bfloat16),
        value_rows,
        preferred_element_type=jnp.float32,
    )
    return (maxima, totals, summed.astype(jnp.bfloat16))


def combine_groups(groups):
    largest = groups[0][0]
    for member in groups[1:]:
        largest = jnp.maximum(largest, member[0])
    totals = 0.0
    summed = 0.0
    for member in groups:
        factor = jnp.exp(member[0] - largest)
        totals = totals + member[1] * factor
        summed = summed + member[2].astype(jnp.float32) * factor[..., None]
    return summed / totals[..., None]


def on_device(
    image_query,
    image_pairs,
    text_query,
    text_pairs,
    text_mask,
    window_offsets,
    timestep,
    gate_table,
):
    rows_dev, width = image_query.shape
    tiles_dev = rows_dev // TILE
    head_count = window_offsets.shape[0]
    head_width = width // head_count
    scaling = 1.0 / math.sqrt(head_width)
    position = lax.axis_index("rows")
    tiles_all = tiles_dev * lax.axis_size("rows")
    first_tile = position * tiles_dev
    reach_back = window_offsets[:, 0]
    reach_ahead = window_offsets[:, 1]
    text_queries, text_gathered = (
        lax.all_gather(text_query, "rows", axis=0, tiled=True),
        lax.all_gather(text_pairs, "rows", axis=1, tiled=True),
    )
    text_keys = text_gathered[0].reshape(-1, head_count, head_width)
    text_values = text_gathered[1].reshape(-1, head_count, head_width)
    text_allowed = (text_mask == 1)[None, None, :]
    queries = image_query.reshape(tiles_dev, TILE, head_count, head_width)
    local_keys = image_pairs[0].reshape(tiles_dev, TILE, head_count, head_width)
    local_values = image_pairs[1].reshape(tiles_dev, TILE, head_count, head_width)

    def permitted(offset):
        target = first_tile + jnp.arange(tiles_dev, dtype=jnp.int32) + offset
        inside = (target >= 0) & (target < tiles_all)
        within = (reach_back <= offset) & (offset <= reach_ahead)
        return (inside[:, None] & within[None, :])[:, None, :, None]

    flat_queries = image_query.reshape(rows_dev, head_count, head_width)
    text_group = attend_rows(flat_queries, text_keys, text_values, text_allowed, scaling)
    text_group = (
        text_group[0].reshape(tiles_dev, TILE, head_count),
        text_group[1].reshape(tiles_dev, TILE, head_count),
        text_group[2].reshape(tiles_dev, TILE, head_count, head_width),
    )
    groups = [attend_tiles(queries, local_keys, local_values, permitted(0), scaling), text_group]
    extended = extended_2(image_pairs, (("rows", 1),), TILE)
    extended = extended.reshape(2, tiles_dev + 2, TILE, head_count, head_width)
    for offset in (-1, 1):
        groups.append(
            attend_tiles(
                queries,
                extended[0, 1 + offset : 1 + offset + tiles_dev],
                extended[1, 1 + offset : 1 + offset + tiles_dev],
                permitted(offset),
                scaling,
            )
        )
    gate_rows = lax.dynamic_index_in_dim(gate_table, timestep[0], 0, keepdims=False)
    attended = combine_groups(groups).reshape(rows_dev, width)
    image_out = (attended * gate_rows[0]).astype(jnp.bfloat16)
    text_flat = text_queries.reshape(-1, head_count, head_width)
    image_keys = image_pairs[0].reshape(rows_dev, head_count, head_width)
    image_values = image_pairs[1].reshape(rows_dev, head_count, head_width)
    every_key = jnp.ones((1, 1, rows_dev), dtype=bool)
    maxima, totals, summed = attend_rows(text_flat, image_keys, image_values, every_key, scaling)
    text_dev = text_query.shape[0]
    text_start = position * text_dev
    global_max = lax.pmax(maxima, "rows")
    factor = jnp.exp(maxima - global_max)
    scaled_summed = summed.astype(jnp.float32) * factor[..., None]
    scaled_totals = totals * factor
    whole_summed, whole_totals = lax.psum((scaled_summed, scaled_totals), "rows")
    shared_summed = lax.dynamic_slice_in_dim(whole_summed, text_start, text_dev, 0)
    shared_totals = lax.dynamic_slice_in_dim(whole_totals, text_start, text_dev, 0)
    remote = (
        lax.dynamic_slice_in_dim(global_max, text_start, text_dev, 0),
        shared_totals,
        shared_summed,
    )
    own_rows = text_query.reshape(text_dev, head_count, head_width)
    own_text = attend_rows(own_rows, text_keys, text_values, text_allowed, scaling)
    text_attended = combine_groups([remote, own_text]).reshape(text_dev, width)
    text_out = (text_attended * gate_rows[1]).astype(jnp.bfloat16)
    return (image_out, text_out)


def solution(mesh):
    placed = (
        P(("groups", "rows"), None),
        P(None, ("groups", "rows"), None),
        P(("groups", "rows"), None),
        P(None, ("groups", "rows"), None),
        P("groups"),
        P(),
        P(),
        P(),
    )
    return jax.shard_map(
        on_device,
        mesh=mesh,
        in_specs=placed,
        out_specs=(P(("groups", "rows"), None), P(("groups", "rows"), None)),
        check_vma=False,
    )
```

profile of v0, /device:TPU:0, one launch (start us, length us, event | category | flops | bytes accessed | tf_op | source)
XLA Modules:
  0.0 297.9 jit_solution(4161448792035331032)
XLA Ops:
  8.0 4.0 %collective-permute-start = (bf16[2,384,2048]{2,1,0:T(8,128)(2,1)}, bf16[2,384,2048]{2,1,0:T(8,128)(2,1)}, u32[]{:S(2)}, u32[]{:S(2)}) collective-permute-start(bf16[2,384,2048]{2,1,0:T(8,128)(2,1)} %param.9), channel_id=1, source_target_pairs={{0,1},{1,2},{2,3},{3,4},{4,5},{5,6},{6,7},{7,8},{8,9},{9,10},{10,1... | collective-permute-start | bytes 9437192 | tf_op jit(solution)/shard_map/ppermute | solution.py:19
  17.3 4.1 %fusion.134 = (bf16[1,384,2048]{2,1,0:T(8,128)(2,1)}, bf16[1,384,2048]{2,1,0:T(8,128)(2,1)}) fusion(bf16[2,384,2048]{2,1,0:T(8,128)(2,1)} %param.9), kind=kLoop, calls=%fused_computation.155 | loop fusion | bytes 6291456 | tf_op jit(solution)/shard_map/slice | solution.py:104
  21.4 1.9 copy.95
  23.2 2.6 copy.57
  25.8 2.5 bitcast_reduce_fusion.2
  28.3 3.6 %copy-done.2 = f32[16,384,384]{2,1,0:T(8,128)} copy-done((f32[16,384,384]{2,1,0:T(8,128)}, f32[16,384,384]{2,1,0:T(8,128)S(1)}, u32[]{:S(2)}) %copy-start.2) | copy-done | bytes 9437208
  31.9 3.5 %fusion.67 = bf16[16,384,128]{1,2,0:T(8,128)(2,1)} fusion(bf16[384,16,128]{0,2,1:T(8,128)(2,1)S(1)} %bitcast.291, f32[16,384,384]{2,1,0:T(8,128)S(1)} %get-tuple-element.26, f32[384,16]{0,1:T(8,128)S(1)} %get-tuple-element.25, pred[16]{0:T(512)(128)(4,1)S(1)} %get-tuple-element.24), kind=kOutput, calls=%fused_computation.81 | convolution fusion | flops 616562688 | bytes 12607504 | tf_op jit(solution)/shard_map/tqhk,tkhe->tqhe/dot_general | solution.py:37
  35.5 28.8 %all-gather.5.cloned.1.call-done = bf16[256,2048]{1,0:T(8,128)(2,1)} async-done(((bf16[16,2048]{1,0:T(8,128)(2,1)}), bf16[256,2048]{1,0:T(8,128)(2,1)}) %all-gather.5.cloned.1.call-update) | async-done | bytes 1048592 | tf_op jit(solution)/shard_map/all_gather | solution.py:97
  64.3 2.3 copy.74
  66.7 4.9 %bitcast_reduce_fusion.3 = (f32[256,16]{0,1:T(8,128)S(1)}, f32[16,384,256]{2,1,0:T(8,128)}) fusion(bf16[384,16,128]{0,2,1:T(8,128)(2,1)S(1)} %bitcast.287, bf16[256,16,128]{0,2,1:T(8,128)(2,1)} %bitcast.294), kind=kOutput, calls=%fused_computation.23 | convolution fusion | flops 405794816 | bytes 8929280 | tf_op jit(solution)/shard_map/qhe,khe->qhk/dot_general | solution.py:48
  71.6 66.7 %pmax.7 = f32[256,16]{0,1:T(8,128)S(1)} all-reduce(f32[256,16]{0,1:T(8,128)S(1)} %get-tuple-element.35), channel_id=1, replica_groups=mesh['groups'=2,'rows'=16] {'rows'}, use_global_device_ids=true, to_apply=%region_9.10 | all-reduce | flops 4096 | bytes 32768 | tf_op jit(solution)/shard_map/pmax | solution.py:143
  138.3 4.0 %fusion.15 = f32[256,16]{0,1:T(8,128)S(1)} fusion(f32[16,384,256]{2,1,0:T(8,128)} %get-tuple-element.36, f32[256,16]{0,1:T(8,128)S(1)} %get-tuple-element.35), kind=kLoop, calls=%fused_computation.30 | loop fusion | flops 4714496 | bytes 6324224 | tf_op jit(solution)/shard_map/reduce_sum | solution.py:53
  142.9 4.4 %bitcast_multiply_fusion.2 = f32[256,16,128]{2,0,1:T(8,128)} fusion(bf16[384,16,128]{0,2,1:T(8,128)(2,1)} %bitcast.290, f32[16,384,256]{2,1,0:T(8,128)S(1)} %copy-done.1, f32[256,16]{0,1:T(8,128)S(1)} %get-tuple-element.35, f32[256,16]{0,1:T(8,128)S(1)} %get-tuple-element.6), kind=kOutput, calls=%fused_computation.79 | convolution fusion | flops 408944640 | bytes 9994240 | tf_op jit(solution)/shard_map/qhk,khe->qhe/dot_general | solution.py:54
  147.3 58.2 %psum.15 = f32[256,16]{0,1:T(8,128)S(1)} all-reduce(f32[256,16]{0,1:T(8,128)S(1)} %get-tuple-element.5), channel_id=1, replica_groups=mesh['groups'=2,'rows'=16] {'rows'}, use_global_device_ids=true, to_apply=%region_13.14 | all-reduce | flops 4096 | bytes 32768 | tf_op jit(solution)/shard_map/psum | solution.py:147
  205.5 7.6 %pad_maximum_fusion = bf16[2,1152,2048]{2,1,0:T(8,128)(2,1)} fusion(bf16[2,384,2048]{2,1,0:T(8,128)(2,1)} %collective-permute-done.1, bf16[2,384,2048]{2,1,0:T(8,128)(2,1)} %param.9, bf16[2,384,2048]{2,1,0:T(8,128)(2,1)} %collective-permute-done), kind=kLoop, calls=%fused_computation | loop fusion | flops 28311552 | bytes 18874368 | tf_op jit(solution)/shard_map/concatenate | solution.py:17
  213.1 11.0 %copy.104 = bf16[288,8,16,128]{3,2,1,0:T(8,128)(2,1)} copy(bf16[288,8,16,128]{3,1,2,0:T(8,128)(2,1)} %bitcast.284) | data formatting | bytes 18874368
  224.2 5.6 %fusion.133 = (bf16[1,1,384,16,128]{4,3,2,1,0:T(8,128)(2,1)}, bf16[1,1,384,16,128]{4,3,2,1,0:T(8,128)(2,1)}, bf16[1,1,384,16,128]{4,3,2,1,0:T(8,128)(2,1)}, bf16[1,1,384,16,128]{4,3,2,1,0:T(8,128)(2,1)S(1)}) fusion(bf16[2,3,384,16,128]{4,3,2,1,0:T(8,128)(2,1)} %bitcast.285), kind=kLoop, calls=%fused_computation.154 | loop fusion | bytes 12582912 | tf_op jit(solution)/shard_map/slice | solution.py:128
  229.8 2.8 copy.99
  232.6 2.0 copy.100
  234.6 3.3 %bitcast_reduce_fusion = (f32[384,16]{0,1:T(8,128)S(1)}, f32[16,384,384]{2,1,0:T(8,128)S(1)}) fusion(pred[16]{0:T(512)(128)(4,1)S(1)} %get-tuple-element.23, bf16[1,1,384,16,128]{4,3,2,1,0:T(8,128)(2,1)} %get-tuple-element.13, bf16[384,2048]{1,0:T(8,128)(2,1)S(1)} %copy-done), kind=kOutput, calls=%fused_computation.2 | convolution fusion | flops 611051520 | bytes 12607504 | tf_op jit(solution)/shard_map/tqhe,tkhe->tqhk/dot_general | solution.py:30
  237.9 2.7 fusion.10
  240.6 3.5 %fusion.73 = bf16[16,128,384]{2,1,0:T(8,128)(2,1)} fusion(f32[16,384,384]{2,1,0:T(8,128)S(1)} %get-tuple-element.28, f32[384,16]{0,1:T(8,128)S(1)} %get-tuple-element.27, pred[16]{0:T(512)(128)(4,1)S(1)} %get-tuple-element.23, bf16[1,1,384,16,128]{2,4,3,1,0:T(8,128)(2,1)S(1)} %copy-done.7), kind=kOutput, calls=%fused_computation.83 | convolution fusion | flops 616562688 | bytes 12607504 | tf_op jit(solution)/shard_map/tqhk,tkhe->tqhe/dot_general | solution.py:37
  244.1 1.9 bitcast_reduce_fusion.1
  246.3 5.5 %fusion.6 = (f32[384,16]{0,1:T(8,128)S(1)}, f32[384,16]{0,1:T(8,128)S(1)}) fusion(f32[16,384,384]{2,1,0:T(8,128)S(1)} %bitcast.283, f32[384,16]{0,1:T(8,128)S(1)} %get-tuple-element.25, pred[16]{0:T(512)(128)(4,1)S(1)} %get-tuple-element.24, f32[384,16]{0,1:T(8,128)S(1)} %get-tuple-element.29, f32[16,384,384]{2,1,0:T(8,128)S(1)} %get-tuple-element.30, ...), kind=kLoop, calls=%fused_computation.16 | loop fusion | flops 23580672 | bytes 18972704 | tf_op jit(solution)/shard_map/reduce_sum | solution.py:36
  251.8 3.5 %fusion.70 = bf16[16,128,384]{2,1,0:T(8,128)(2,1)} fusion(f32[16,384,384]{2,1,0:T(8,128)S(1)} %get-tuple-element.30, f32[384,16]{0,1:T(8,128)S(1)} %get-tuple-element.29, pred[16]{0:T(512)(128)(4,1)S(1)} %get-tuple-element.22, bf16[1,1,384,16,128]{2,4,3,1,0:T(8,128)(2,1)S(1)} %copy-done.6), kind=kOutput, calls=%fused_computation.82 | convolution fusion | flops 616562688 | bytes 12607504 | tf_op jit(solution)/shard_map/tqhk,tkhe->tqhe/dot_general | solution.py:37
  255.4 6.8 %fusion.135 = (bf16[1,256,2048]{2,0,1:T(2,128)(2,1)}, bf16[1,256,2048]{2,0,1:T(2,128)(2,1)}) fusion(bf16[2,256,2048]{2,0,1:T(2,128)(2,1)} %all-gather.3.cloned.1.call-done), kind=kLoop, calls=%fused_computation.156 | loop fusion | bytes 4194304 | tf_op jit(solution)/shard_map/slice | solution.py:101
  262.2 5.8 %copy.67 = bf16[1,256,2048]{1,2,0:T(8,128)(2,1)} copy(bf16[1,256,2048]{2,0,1:T(2,128)(2,1)} %get-tuple-element.18) | data formatting | bytes 2097152 | tf_op jit(solution)/shard_map/slice | solution.py:101
  268.0 4.8 %copy.96 = bf16[1,256,2048]{1,2,0:T(8,128)(2,1)S(1)} copy(bf16[1,256,2048]{2,0,1:T(2,128)(2,1)} %get-tuple-element.19) | data formatting | bytes 2097152
  274.2 1.7 fusion.44
  276.9 4.5 %fusion.52 = f32[1,384,16,128]{1,3,2,0:T(8,128)} fusion(bf16[16,384,128]{1,2,0:T(8,128)(2,1)S(1)} %copy-done.10, bf16[16,128,384]{2,1,0:T(8,128)(2,1)S(1)} %copy-done.11, bf16[16,128,384]{2,1,0:T(8,128)(2,1)S(1)} %copy-done.12, f32[384,16]{0,1:T(8,128)S(1)} %get-tuple-element.7, f32[384,16]{0,1:T(8,128)S(1)} %get-tuple-element.11, ...), kind=kOutput, calls=%fused_computation.63 | convolution fusion | flops 420741120 | bytes 15352064 | tf_op jit(solution)/shard_map/qhk,khe->qhe/dot_general | solution.py:54
  281.4 3.6 %copy.73 = f32[384,2048]{1,0:T(8,128)} copy(f32[384,2048]{0,1:T(8,128)} %bitcast.295) | data formatting | bytes 6291456 | tf_op jit(solution)/shard_map/reshape | solution.py:134
  288.0 3.4 %multiply_convert_fusion = bf16[384,2048]{1,0:T(8,128)(2,1)} fusion(f32[384,2048]{1,0:T(8,128)} %copy.73, f32[2048]{0:T(1024)S(1)} %bitcast.296), kind=kLoop, calls=%fused_computation.72 | loop fusion | flops 1572864 | bytes 4726784 | tf_op jit(solution)/shard_map/convert_element_type | solution.py:135
  (55 shorter events, 11.6 us)
Async XLA Ops:
  7.2 18.7 %copy-start = (bf16[384,2048]{1,0:T(8,128)(2,1)S(1)}, bf16[384,2048]{1,0:T(8,128)(2,1)}, u32[]{:S(2)}) copy-start(bf16[384,2048]{1,0:T(8,128)(2,1)} %param.8) | copy-start | bytes 4718596
  7.2 57.1 %all-gather.5.cloned.1.call-start = ((), (), s32[]{:S(2)}) async-start(), calls=%async_computation.1 | async-start | bytes 1114112 | tf_op jit(solution)/shard_map/all_gather | solution.py:97
  7.9 247.5 %all-gather.3.cloned.1.call-start = ((), (), s32[]{:S(2)}) async-start(), calls=%async_computation | async-start | bytes 2228224 | tf_op jit(solution)/shard_map/all_gather | solution.py:98
  8.0 197.5 %collective-permute-start = (bf16[2,384,2048]{2,1,0:T(8,128)(2,1)}, bf16[2,384,2048]{2,1,0:T(8,128)(2,1)}, u32[]{:S(2)}, u32[]{:S(2)}) collective-permute-start(bf16[2,384,2048]{2,1,0:T(8,128)(2,1)} %param.9), channel_id=1, source_target_pairs={{0,1},{1,2},{2,3},{3,4},{4,5},{5,6},{6,7},{7,8},{8,9},{9,10},{10,1... | collective-permute-start | bytes 9437192 | tf_op jit(solution)/shard_map/ppermute | solution.py:19
  12.0 193.5 %collective-permute-start.1 = (bf16[2,384,2048]{2,1,0:T(8,128)(2,1)}, bf16[2,384,2048]{2,1,0:T(8,128)(2,1)}, u32[]{:S(2)}, u32[]{:S(2)}) collective-permute-start(bf16[2,384,2048]{2,1,0:T(8,128)(2,1)} %param.9), channel_id=1, source_target_pairs={{1,0},{2,1},{3,2},{4,3},{5,4},{6,5},{7,6},{8,7},{9,8},{10,9},{11,1... | collective-permute-start | bytes 9437192 | tf_op jit(solution)/shard_map/ppermute | solution.py:21
  15.0 270.7 %all-reduce.2.cloned.1.call-start = ((), (), s32[]{:S(2)}) async-start(), calls=%async_computation.2 | async-start | bytes 4194304 | tf_op jit(solution)/shard_map/psum | solution.py:147
  17.3 4.1 %copy-start.9 = (s32[256]{0:T(256)S(1)}, s32[256]{0:T(256)}, u32[]{:S(2)}) copy-start(s32[256]{0:T(256)} %param.12) | copy-start | bytes 3076
  25.8 6.1 %copy-start.3 = (bf16[1,384,2048]{1,2,0:T(8,128)(2,1)S(1)}, bf16[1,384,2048]{1,2,0:T(8,128)(2,1)}, u32[]{:S(2)}) copy-start(bf16[1,384,2048]{1,2,0:T(8,128)(2,1)} %copy.57) | copy-start | bytes 4718596
  28.3 3.6 %copy-start.2 = (f32[16,384,384]{2,1,0:T(8,128)}, f32[16,384,384]{2,1,0:T(8,128)S(1)}, u32[]{:S(2)}) copy-start(f32[16,384,384]{2,1,0:T(8,128)S(1)} %get-tuple-element.26) | copy-start | bytes 28311556
  138.3 4.6 %copy-start.1 = (f32[16,384,256]{2,1,0:T(8,128)S(1)}, f32[16,384,256]{2,1,0:T(8,128)}, u32[]{:S(2)}) copy-start(f32[16,384,256]{2,1,0:T(8,128)} %get-tuple-element.36) | copy-start | bytes 18874372
  237.9 2.7 copy-start.7
  240.6 3.5 %copy-start.5 = (bf16[1,1,384,16,128]{4,3,2,1,0:T(8,128)(2,1)S(1)}, bf16[1,1,384,16,128]{4,3,2,1,0:T(8,128)(2,1)}, u32[]{:S(2)}) copy-start(bf16[1,1,384,16,128]{4,3,2,1,0:T(8,128)(2,1)} %get-tuple-element.14) | copy-start | bytes 4718596
  240.6 5.4 %slice-start = ((s8[9437184]{0:T(1024)(128)(4,1)}), s8[4194304]{0:T(1024)(128)(4,1)S(1)}, s32[]{:S(2)}) async-start(s8[9437184]{0:T(1024)(128)(4,1)} %bitcast.282), calls=%async_computation.3 | async-start | bytes 8388608
  240.6 5.4 %slice-start.1 = ((s8[9437184]{0:T(1024)(128)(4,1)}), s8[1048576]{0:T(1024)(128)(4,1)S(1)}, s32[]{:S(2)}) async-start(s8[9437184]{0:T(1024)(128)(4,1)} %bitcast.282), calls=%async_computation.4 | async-start | bytes 2097152
  244.1 2.2 slice-start.2
  246.3 5.5 %copy-start.6 = (bf16[1,1,384,16,128]{2,4,3,1,0:T(8,128)(2,1)S(1)}, bf16[1,1,384,16,128]{2,4,3,1,0:T(8,128)(2,1)}, u32[]{:S(2)}) copy-start(bf16[1,1,384,16,128]{2,4,3,1,0:T(8,128)(2,1)} %copy.99) | copy-start | bytes 4718596
  274.2 1.8 copy-start.4
  274.2 1.8 copy-start.10
  274.2 2.2 copy-start.11
  274.2 2.7 copy-start.12
  281.4 3.6 %copy-start.8 = (bf16[16,2048]{1,0:T(8,128)(2,1)S(1)}, bf16[16,2048]{1,0:T(8,128)(2,1)}, u32[]{:S(2)}) copy-start(bf16[16,2048]{1,0:T(8,128)(2,1)} %param.10) | copy-start | bytes 196612
Sparse Core Ops, SparseCore 0:
  10.2 54.0 all-gather.4
  66.5 43.8 all-gather.2
  147.5 95.1 all-reduce.1
where the time goes:
time: 299 us; the launch traced here: 298 us
  blocking collectives  125 us (42%)
  local copies, waits for them, and re-layouts  61.2 us (20%)
  matrix products  35.5 us (12%)
  waiting for transfers between devices  29.6 us (10%)
  other arithmetic  26.6 us (9%)
  between operations  14.7 us (5%)
  starting transfers between devices  5.42 us (2%)
    pmax x1, blocking collectives, on_device(): global_max = lax.pmax(maxima, 'rows')  66.7 us
    psum x1, blocking collectives, on_device(): lax.psum((scaled_summed, scaled_totals), 'rows')  58.2 us
    unnamed x38, local copies, waits for them, and re-layouts  29.6 us
    all_gather x1, waiting for transfers between devices, on_device(): lax.all_gather(text_query, 'rows', axis=0, tiled=True)  28.8 us
    slice x2, local copies, waits for them, and re-layouts, on_device(): text_values = text_gathered[1].reshape(-1, head_count, head_width)  12.6 us
    dot_general x3, matrix products, attend_tiles(): jnp.einsum('tqhk,tkhe->tqhe', exponent.astype(jnp.bfloat16), value_rows,...  10.6 us
    dot_general x3, matrix products, attend_rows(): jnp.einsum('qhk,khe->qhe', exponent.astype(jnp.bfloat16), value_rows, pre...  10.5 us
    reduce_sum x2, other arithmetic, attend_tiles(): totals = jnp.sum(exponent, axis=-1)  8.14 us
  transfers between devices with their start and end apart: 5, of which 1 were waited for; matrix products, arithmetic and copies ran while one was open for 38% of the time, Pallas kernels for 0%

commit v1 on v0

--- a/solution.py
+++ b/solution.py
@@ -6,6 +6,18 @@
 
 TILE = 384
 masked_score = -1e30
+
+
+def doubled_up(x, axis, dim):
+    ways, here = (lax.axis_size(axis), lax.axis_index(axis))
+    grown, reach = (x, 1)
+    while reach < ways:
+        theirs = lax.ppermute(grown, axis, [(d, d ^ reach) for d in range(ways)])
+        mine_first = jnp.concatenate([grown, theirs], axis=dim)
+        theirs_first = jnp.concatenate([theirs, grown], axis=dim)
+        grown = jnp.where(here & reach == 0, mine_first, theirs_first)
+        reach = 2 * reach
+    return grown
 
 
 def extended_2(cells, sides, width):
@@ -94,7 +106,7 @@
     reach_back = window_offsets[:, 0]
     reach_ahead = window_offsets[:, 1]
     text_queries, text_gathered = (
-        lax.all_gather(text_query, "rows", axis=0, tiled=True),
+        doubled_up(text_query, "rows", 0),
         lax.all_gather(text_pairs, "rows", axis=1, tiled=True),
     )
     text_keys = text_gathered[0].reshape(-1, head_count, head_width)

time: 299 us -> 348 us (1.16)
  starting transfers between devices: 5.42 us -> 44.7 us
  waiting for transfers between devices: 29.6 us -> 50.8 us
  blocking collectives: 125 us -> 119 us
  local copies, waits for them, and re-layouts: 61.2 us -> 56.4 us
    ppermute x0 -> x4, waiting for transfers between devices: none -> 50.7 us  [doubled_up(): theirs = lax.ppermute(grown, axis, [(d, d ^ reach) for d in range(ways)])]
    ppermute x0 -> x4, starting transfers between devices: none -> 39.1 us  [doubled_up(): theirs = lax.ppermute(grown, axis, [(d, d ^ reach) for d in range(ways)])]
    all_gather x1 -> x0, waiting for transfers between devices: 28.8 us -> none  [on_device(): lax.all_gather(text_query, 'rows', axis=0, tiled=True)]
    pmax x1, blocking collectives: 66.7 us -> 60.9 us  [on_device(): global_max = lax.pmax(maxima, 'rows')]
    unnamed x38 -> x40, local copies, waits for them, and re-layouts: 29.6 us -> 26 us
  transfers between devices with their start and end apart: 5 -> 8, of which waited for: 1 -> 3; matrix products, arithmetic and copies ran while one was open for 38% -> 32% of each run, Pallas kernels for 0% -> 0%
where the time goes in v1:
time: 348 us; the launch traced here: 347 us
  blocking collectives  119 us (34%)
  local copies, waits for them, and re-layouts  56.4 us (16%)
  waiting for transfers between devices  50.8 us (15%)
  starting transfers between devices  44.7 us (13%)
  matrix products  34.3 us (10%)
  other arithmetic  26.3 us (8%)
  between operations  15.1 us (4%)
    pmax x1, blocking collectives, on_device(): global_max = lax.pmax(maxima, 'rows')  60.9 us
    psum x1, blocking collectives, on_device(): lax.psum((scaled_summed, scaled_totals), 'rows')  58.2 us
    ppermute x4, waiting for transfers between devices, doubled_up(): theirs = lax.ppermute(grown, axis, [(d, d ^ reach) for d in range(ways)])  50.7 us
    ppermute x4, starting transfers between devices, doubled_up(): theirs = lax.ppermute(grown, axis, [(d, d ^ reach) for d in range(ways)])  39.1 us
    unnamed x40, local copies, waits for them, and re-layouts  26 us
    slice x2, local copies, waits for them, and re-layouts, on_device(): text_values = text_gathered[1].reshape(-1, head_count, head_width)  12.7 us
    dot_general x3, matrix products, attend_tiles(): jnp.einsum('tqhk,tkhe->tqhe', exponent.astype(jnp.bfloat16), value_rows,...  11.2 us
    dot_general x3, matrix products, attend_rows(): jnp.einsum('qhk,khe->qhe', exponent.astype(jnp.bfloat16), value_rows, pre...  10 us
  transfers between devices with their start and end apart: 8, of which 3 were waited for; matrix products, arithmetic and copies ran while one was open for 32% of the time, Pallas kernels for 0%

profile of v1, /device:TPU:0, one launch (start us, length us, event | category | flops | bytes accessed | tf_op | source)
XLA Modules:
  0.0 346.7 jit_solution(11941241099091726124)
XLA Ops:
  7.2 4.2 %collective-permute-start = (bf16[2,384,2048]{2,1,0:T(8,128)(2,1)}, bf16[2,384,2048]{2,1,0:T(8,128)(2,1)}, u32[]{:S(2)}, u32[]{:S(2)}) collective-permute-start(bf16[2,384,2048]{2,1,0:T(8,128)(2,1)} %param.9), channel_id=1, source_target_pairs={{0,1},{1,2},{2,3},{3,4},{4,5},{5,6},{6,7},{7,8},{8,9},{9,10},{10,1... | collective-permute-start | bytes 9437192 | tf_op jit(solution)/shard_map/ppermute | solution.py:31
  17.0 4.1 %fusion.140 = (bf16[1,384,2048]{2,1,0:T(8,128)(2,1)}, bf16[1,384,2048]{2,1,0:T(8,128)(2,1)}) fusion(bf16[2,384,2048]{2,1,0:T(8,128)(2,1)} %param.9), kind=kLoop, calls=%fused_computation.173 | loop fusion | bytes 6291456 | tf_op jit(solution)/shard_map/slice | solution.py:116
  21.7 1.9 copy.116
  23.6 2.6 copy.73
  26.2 2.5 bitcast_reduce_fusion.2
  28.8 4.1 %fusion.67 = bf16[16,384,128]{1,2,0:T(8,128)(2,1)} fusion(bf16[384,16,128]{0,2,1:T(8,128)(2,1)S(1)} %bitcast.311, f32[16,384,384]{2,1,0:T(8,128)S(1)} %get-tuple-element.26, f32[384,16]{0,1:T(8,128)S(1)} %get-tuple-element.25, pred[16]{0:T(512)(128)(4,1)S(1)} %get-tuple-element.24), kind=kOutput, calls=%fused_computation.81 | convolution fusion | flops 616562688 | bytes 12607504 | tf_op jit(solution)/shard_map/tqhk,tkhe->tqhe/dot_general | solution.py:49
  35.5 25.7 %collective-permute-done.3 = bf16[32,2048]{1,0:T(8,128)(2,1)S(1)} collective-permute-done((bf16[32,2048]{1,0:T(8,128)(2,1)S(1)}, bf16[32,2048]{1,0:T(8,128)(2,1)S(1)}, u32[]{:S(2)}, u32[]{:S(2)}) %collective-permute-start.3) | collective-permute-done | bytes 131104 | tf_op jit(solution)/shard_map/ppermute | solution.py:15
  61.2 32.5 %collective-permute-start.4 = (bf16[64,2048]{1,0:T(8,128)(2,1)S(1)}, bf16[64,2048]{1,0:T(8,128)(2,1)S(1)}, u32[]{:S(2)}, u32[]{:S(2)}) collective-permute-start(bf16[64,2048]{1,0:T(8,128)(2,1)S(1)} %maximum_select_fusion.5), channel_id=1, source_target_pairs={{0,4},{1,5},{2,6},{3,7},{4,0},{5,1},{6,2},{7,3},{8,12},{9,13},{10,... | collective-permute-start | bytes 786440 | tf_op jit(solution)/shard_map/ppermute | solution.py:15
  93.8 4.8 %collective-permute-done.4 = bf16[64,2048]{1,0:T(8,128)(2,1)S(1)} collective-permute-done((bf16[64,2048]{1,0:T(8,128)(2,1)S(1)}, bf16[64,2048]{1,0:T(8,128)(2,1)S(1)}, u32[]{:S(2)}, u32[]{:S(2)}) %collective-permute-start.4) | collective-permute-done | bytes 262176 | tf_op jit(solution)/shard_map/ppermute | solution.py:15
  98.7 3.2 collective-permute-start.5
  102.3 20.2 %collective-permute-done.5 = bf16[128,2048]{1,0:T(8,128)(2,1)S(1)} collective-permute-done((bf16[128,2048]{1,0:T(8,128)(2,1)S(1)}, bf16[128,2048]{1,0:T(8,128)(2,1)S(1)}, u32[]{:S(2)}, u32[]{:S(2)}) %collective-permute-start.5) | collective-permute-done | bytes 524320 | tf_op jit(solution)/shard_map/ppermute | solution.py:15
  122.7 3.7 %bitcast_reduce_fusion.3 = (f32[256,16]{0,1:T(8,128)S(1)}, f32[16,256,384]{2,1,0:T(8,128)}) fusion(bf16[384,16,128]{0,2,1:T(8,128)(2,1)S(1)} %bitcast.307, bf16[128,16,128]{2,0,1:T(8,128)(2,1)S(1)} %copy_bitcast_fusion.4, bf16[128,16,128]{2,0,1:T(8,128)(2,1)S(1)} %maximum_select_fusion.2, pred[]{:T(512)S(6)} %eq.20), kind=kOutput, calls=%fused_computation.23 | convolution fusion | flops 410513408 | bytes 8929281 | tf_op jit(solution)/shard_map/qhe,khe->qhk/dot_general | solution.py:60
  126.3 60.9 %pmax.7 = f32[256,16]{0,1:T(8,128)S(1)} all-reduce(f32[256,16]{0,1:T(8,128)S(1)} %get-tuple-element.35), channel_id=1, replica_groups=mesh['groups'=2,'rows'=16] {'rows'}, use_global_device_ids=true, to_apply=%region_9.10 | all-reduce | flops 4096 | bytes 32768 | tf_op jit(solution)/shard_map/pmax | solution.py:155
  187.3 4.0 %fusion.15 = f32[256,16]{0,1:T(8,128)S(1)} fusion(f32[16,256,384]{2,1,0:T(8,128)} %get-tuple-element.36, f32[256,16]{0,1:T(8,128)S(1)} %get-tuple-element.35), kind=kLoop, calls=%fused_computation.30 | loop fusion | flops 4714496 | bytes 6324224 | tf_op jit(solution)/shard_map/reduce_sum | solution.py:65
  191.9 3.9 %bitcast_multiply_fusion.2 = f32[256,16,128]{2,0,1:T(8,128)} fusion(bf16[384,16,128]{0,2,1:T(8,128)(2,1)} %bitcast.310, f32[16,256,384]{2,1,0:T(8,128)S(1)} %copy-done.1, f32[256,16]{0,1:T(8,128)S(1)} %get-tuple-element.35, f32[256,16]{0,1:T(8,128)S(1)} %get-tuple-element.6), kind=kOutput, calls=%fused_computation.79 | convolution fusion | flops 408944640 | bytes 9994240 | tf_op jit(solution)/shard_map/qhk,khe->qhe/dot_general | solution.py:66
  195.8 58.2 %psum.15 = f32[256,16]{0,1:T(8,128)S(1)} all-reduce(f32[256,16]{0,1:T(8,128)S(1)} %get-tuple-element.5), channel_id=1, replica_groups=mesh['groups'=2,'rows'=16] {'rows'}, use_global_device_ids=true, to_apply=%region_13.14 | all-reduce | flops 4096 | bytes 32768 | tf_op jit(solution)/shard_map/psum | solution.py:159
  254.1 7.6 %pad_maximum_fusion = bf16[2,1152,2048]{2,1,0:T(8,128)(2,1)} fusion(bf16[2,384,2048]{2,1,0:T(8,128)(2,1)} %collective-permute-done.1, bf16[2,384,2048]{2,1,0:T(8,128)(2,1)} %param.9, bf16[2,384,2048]{2,1,0:T(8,128)(2,1)} %collective-permute-done), kind=kLoop, calls=%fused_computation | loop fusion | flops 28311552 | bytes 18874368 | tf_op jit(solution)/shard_map/concatenate | solution.py:29
  261.7 11.0 %copy.129 = bf16[288,8,16,128]{3,2,1,0:T(8,128)(2,1)} copy(bf16[288,8,16,128]{3,1,2,0:T(8,128)(2,1)} %bitcast.304) | data formatting | bytes 18874368
  272.7 5.6 %fusion.139 = (bf16[1,1,384,16,128]{4,3,2,1,0:T(8,128)(2,1)}, bf16[1,1,384,16,128]{4,3,2,1,0:T(8,128)(2,1)}, bf16[1,1,384,16,128]{4,3,2,1,0:T(8,128)(2,1)}, bf16[1,1,384,16,128]{4,3,2,1,0:T(8,128)(2,1)S(1)}) fusion(bf16[2,3,384,16,128]{4,3,2,1,0:T(8,128)(2,1)} %bitcast.305), kind=kLoop, calls=%fused_computation.172 | loop fusion | bytes 12582912 | tf_op jit(solution)/shard_map/slice | solution.py:140
  278.3 2.8 copy.120
  281.2 2.0 copy.121
  283.2 3.3 bitcast_reduce_fusion
  286.5 2.7 fusion.10
  289.2 3.5 %fusion.73 = bf16[16,128,384]{2,1,0:T(8,128)(2,1)} fusion(f32[16,384,384]{2,1,0:T(8,128)S(1)} %get-tuple-element.28, f32[384,16]{0,1:T(8,128)S(1)} %get-tuple-element.27, pred[16]{0:T(512)(128)(4,1)S(1)} %get-tuple-element.23, bf16[1,1,384,16,128]{2,4,3,1,0:T(8,128)(2,1)S(1)} %copy-done.7), kind=kOutput, calls=%fused_computation.83 | convolution fusion | flops 616562688 | bytes 12607504 | tf_op jit(solution)/shard_map/tqhk,tkhe->tqhe/dot_general | solution.py:49
  294.9 5.5 %fusion.6 = (f32[384,16]{0,1:T(8,128)S(1)}, f32[384,16]{0,1:T(8,128)S(1)}) fusion(f32[16,384,384]{2,1,0:T(8,128)S(1)} %bitcast.303, f32[384,16]{0,1:T(8,128)S(1)} %get-tuple-element.25, pred[16]{0:T(512)(128)(4,1)S(1)} %get-tuple-element.24, f32[384,16]{0,1:T(8,128)S(1)} %get-tuple-element.29, f32[16,384,384]{2,1,0:T(8,128)S(1)} %get-tuple-element.30, ...), kind=kLoop, calls=%fused_computation.16 | loop fusion | flops 23580672 | bytes 18972704 | tf_op jit(solution)/shard_map/reduce_sum | solution.py:48
  300.4 3.6 %fusion.70 = bf16[16,128,384]{2,1,0:T(8,128)(2,1)} fusion(f32[16,384,384]{2,1,0:T(8,128)S(1)} %get-tuple-element.30, f32[384,16]{0,1:T(8,128)S(1)} %get-tuple-element.29, pred[16]{0:T(512)(128)(4,1)S(1)} %get-tuple-element.22, bf16[1,1,384,16,128]{2,4,3,1,0:T(8,128)(2,1)S(1)} %copy-done.6), kind=kOutput, calls=%fused_computation.82 | convolution fusion | flops 616562688 | bytes 12607504 | tf_op jit(solution)/shard_map/tqhk,tkhe->tqhe/dot_general | solution.py:49
  303.9 6.9 %fusion.141 = (bf16[1,256,2048]{2,0,1:T(2,128)(2,1)}, bf16[1,256,2048]{2,0,1:T(2,128)(2,1)}) fusion(bf16[2,256,2048]{2,0,1:T(2,128)(2,1)} %all-gather.2.cloned.1.call-done), kind=kLoop, calls=%fused_computation.174 | loop fusion | bytes 4194304 | tf_op jit(solution)/shard_map/slice | solution.py:113
  310.8 5.8 %copy.83 = bf16[1,256,2048]{1,2,0:T(8,128)(2,1)} copy(bf16[1,256,2048]{2,0,1:T(2,128)(2,1)} %get-tuple-element.18) | data formatting | bytes 2097152 | tf_op jit(solution)/shard_map/slice | solution.py:113
  316.6 4.8 %copy.117 = bf16[1,256,2048]{1,2,0:T(8,128)(2,1)S(1)} copy(bf16[1,256,2048]{2,0,1:T(2,128)(2,1)} %get-tuple-element.19) | data formatting | bytes 2097152
  325.5 4.5 %fusion.52 = f32[1,384,16,128]{1,3,2,0:T(8,128)} fusion(bf16[16,384,128]{1,2,0:T(8,128)(2,1)S(1)} %copy-done.11, bf16[16,128,384]{2,1,0:T(8,128)(2,1)S(1)} %copy-done.12, bf16[16,128,384]{2,1,0:T(8,128)(2,1)S(1)} %copy-done.13, f32[384,16]{0,1:T(8,128)S(1)} %get-tuple-element.7, f32[384,16]{0,1:T(8,128)S(1)} %get-tuple-element.11, ...), kind=kOutput, calls=%fused_computation.63 | convolution fusion | flops 420741120 | bytes 15352064 | tf_op jit(solution)/shard_map/qhk,khe->qhe/dot_general | solution.py:66
  330.0 3.6 %copy.89 = f32[384,2048]{1,0:T(8,128)} copy(f32[384,2048]{0,1:T(8,128)} %bitcast.314) | data formatting | bytes 6291456 | tf_op jit(solution)/shard_map/reshape | solution.py:146
  336.5 3.4 multiply_convert_fusion
  (72 shorter events, 18.7 us)
Async XLA Ops:
  7.2 19.0 %copy-start = (bf16[384,2048]{1,0:T(8,128)(2,1)S(1)}, bf16[384,2048]{1,0:T(8,128)(2,1)}, u32[]{:S(2)}) copy-start(bf16[384,2048]{1,0:T(8,128)(2,1)} %param.8) | copy-start | bytes 4718596
  7.2 296.8 %all-gather.2.cloned.1.call-start = ((), (), s32[]{:S(2)}) async-start(), calls=%async_computation | async-start | bytes 2228224 | tf_op jit(solution)/shard_map/all_gather | solution.py:110
  7.2 246.8 %collective-permute-start = (bf16[2,384,2048]{2,1,0:T(8,128)(2,1)}, bf16[2,384,2048]{2,1,0:T(8,128)(2,1)}, u32[]{:S(2)}, u32[]{:S(2)}) collective-permute-start(bf16[2,384,2048]{2,1,0:T(8,128)(2,1)} %param.9), channel_id=1, source_target_pairs={{0,1},{1,2},{2,3},{3,4},{4,5},{5,6},{6,7},{7,8},{8,9},{9,10},{10,1... | collective-permute-start | bytes 9437192 | tf_op jit(solution)/shard_map/ppermute | solution.py:31
  11.4 242.7 %collective-permute-start.1 = (bf16[2,384,2048]{2,1,0:T(8,128)(2,1)}, bf16[2,384,2048]{2,1,0:T(8,128)(2,1)}, u32[]{:S(2)}, u32[]{:S(2)}) collective-permute-start(bf16[2,384,2048]{2,1,0:T(8,128)(2,1)} %param.9), channel_id=1, source_target_pairs={{1,0},{2,1},{3,2},{4,3},{5,4},{6,5},{7,6},{8,7},{9,8},{10,9},{11,1... | collective-permute-start | bytes 9437192 | tf_op jit(solution)/shard_map/ppermute | solution.py:33
  12.7 21.0 %collective-permute-start.2 = (bf16[16,2048]{1,0:T(8,128)(2,1)}, bf16[16,2048]{1,0:T(8,128)(2,1)S(1)}, u32[]{:S(2)}, u32[]{:S(2)}) collective-permute-start(bf16[16,2048]{1,0:T(8,128)(2,1)} %param.10), channel_id=1, source_target_pairs={{0,1},{1,0},{2,3},{3,2},{4,5},{5,4},{6,7},{7,6},{8,9},{9,8},{10,11... | collective-permute-start | bytes 196616 | tf_op jit(solution)/shard_map/ppermute | solution.py:15
  16.1 318.1 %all-reduce.2.cloned.1.call-start = ((), (), s32[]{:S(2)}) async-start(), calls=%async_computation.1 | async-start | bytes 4194304 | tf_op jit(solution)/shard_map/psum | solution.py:159
  21.7 4.5 %copy-start.9 = (s32[16,2]{0,1:T(2,128)S(1)}, s32[16,2]{0,1:T(2,128)}, u32[]{:S(2)}) copy-start(s32[16,2]{0,1:T(2,128)} %param.13) | copy-start | bytes 388
  26.2 2.5 copy-start.3
  28.7 4.2 %copy-start.2 = (f32[16,384,384]{2,1,0:T(8,128)}, f32[16,384,384]{2,1,0:T(8,128)S(1)}, u32[]{:S(2)}) copy-start(f32[16,384,384]{2,1,0:T(8,128)S(1)} %get-tuple-element.26) | copy-start | bytes 28311556
  28.7 5.0 %copy-start.8 = (bf16[16,2048]{1,0:T(8,128)(2,1)S(1)}, bf16[16,2048]{1,0:T(8,128)(2,1)}, u32[]{:S(2)}) copy-start(bf16[16,2048]{1,0:T(8,128)(2,1)} %param.10) | copy-start | bytes 196612
  28.7 6.7 %copy-start.10 = (s32[256]{0:T(256)S(1)}, s32[256]{0:T(256)}, u32[]{:S(2)}) copy-start(s32[256]{0:T(256)} %param.12) | copy-start | bytes 3076
  33.8 27.4 %collective-permute-start.3 = (bf16[32,2048]{1,0:T(8,128)(2,1)S(1)}, bf16[32,2048]{1,0:T(8,128)(2,1)S(1)}, u32[]{:S(2)}, u32[]{:S(2)}) collective-permute-start(bf16[32,2048]{1,0:T(8,128)(2,1)S(1)} %maximum_select_fusion.7), channel_id=1, source_target_pairs={{0,2},{1,3},{2,0},{3,1},{4,6},{5,7},{6,4},{7,5},{8,10},{9,11},{10,... | collective-permute-start | bytes 393224 | tf_op jit(solution)/shard_map/ppermute | solution.py:15
  61.2 37.4 %collective-permute-start.4 = (bf16[64,2048]{1,0:T(8,128)(2,1)S(1)}, bf16[64,2048]{1,0:T(8,128)(2,1)S(1)}, u32[]{:S(2)}, u32[]{:S(2)}) collective-permute-start(bf16[64,2048]{1,0:T(8,128)(2,1)S(1)} %maximum_select_fusion.5), channel_id=1, source_target_pairs={{0,4},{1,5},{2,6},{3,7},{4,0},{5,1},{6,2},{7,3},{8,12},{9,13},{10,... | collective-permute-start | bytes 786440 | tf_op jit(solution)/shard_map/ppermute | solution.py:15
  98.7 23.8 %collective-permute-start.5 = (bf16[128,2048]{1,0:T(8,128)(2,1)S(1)}, bf16[128,2048]{1,0:T(8,128)(2,1)S(1)}, u32[]{:S(2)}, u32[]{:S(2)}) collective-permute-start(bf16[128,2048]{1,0:T(8,128)(2,1)S(1)} %maximum_select_fusion.3), channel_id=1, source_target_pairs={{0,8},{1,9},{2,10},{3,11},{4,12},{5,13},{6,14},{7,15},{8,0},{9,1},... | collective-permute-start | bytes 1572872 | tf_op jit(solution)/shard_map/ppermute | solution.py:15
  187.3 4.6 %copy-start.1 = (f32[16,256,384]{2,1,0:T(8,128)S(1)}, f32[16,256,384]{2,1,0:T(8,128)}, u32[]{:S(2)}) copy-start(f32[16,256,384]{2,1,0:T(8,128)} %get-tuple-element.36) | copy-start | bytes 18874372
  286.5 2.7 copy-start.7
  289.2 3.5 %copy-start.5 = (bf16[1,1,384,16,128]{4,3,2,1,0:T(8,128)(2,1)S(1)}, bf16[1,1,384,16,128]{4,3,2,1,0:T(8,128)(2,1)}, u32[]{:S(2)}) copy-start(bf16[1,1,384,16,128]{4,3,2,1,0:T(8,128)(2,1)} %get-tuple-element.14) | copy-start | bytes 4718596
  289.2 5.4 %slice-start = ((s8[9437184]{0:T(1024)(128)(4,1)}), s8[4194304]{0:T(1024)(128)(4,1)S(1)}, s32[]{:S(2)}) async-start(s8[9437184]{0:T(1024)(128)(4,1)} %bitcast.302), calls=%async_computation.2 | async-start | bytes 8388608
  289.2 5.4 %slice-start.1 = ((s8[9437184]{0:T(1024)(128)(4,1)}), s8[1048576]{0:T(1024)(128)(4,1)S(1)}, s32[]{:S(2)}) async-start(s8[9437184]{0:T(1024)(128)(4,1)} %bitcast.302), calls=%async_computation.3 | async-start | bytes 2097152
  292.7 2.2 slice-start.2
  294.9 5.5 %copy-start.6 = (bf16[1,1,384,16,128]{2,4,3,1,0:T(8,128)(2,1)S(1)}, bf16[1,1,384,16,128]{2,4,3,1,0:T(8,128)(2,1)}, u32[]{:S(2)}) copy-start(bf16[1,1,384,16,128]{2,4,3,1,0:T(8,128)(2,1)} %copy.120) | copy-start | bytes 4718596
  322.8 1.8 copy-start.4
  322.8 1.8 copy-start.11
  322.8 2.2 copy-start.12
  322.8 2.7 copy-start.13
Sparse Core Ops, SparseCore 0:
  16.2 53.8 all-gather.1
  195.9 95.2 all-reduce.1
